TPU v7x, 32 devices: a whole 2x2x4 slice. The times are simulated.
32 devices in a mesh: gx: 8 (over z, y), gy: 4 (over x, core).
Axes of the slice: x: 2, y: 2, z: 4, core: 2. Of those that a mesh axis runs over, the one named last changes fastest.
Arguments:
- embeds: bfloat16 [32, 2048, 768], P('gx', 'gy'), may hold values from -6 to 6
- fetch_list: int32 [2, 8, 8], replicated, may hold values from 0 to 2047, as said below
- partners: int32 [2, 8, 8, 2], replicated, may hold values from 0 to 31, as said below
- counts: int32 [32], replicated, may hold values from 512 to 2048
Outputs:
- nearest: float32 [32, 2048], P('gx', 'gy')
Inputs may be any that keep to these rules, and one draw needn't show every extreme that they name: fetch_list[w, h, g] // 64 is a block stored by index g of gx, that is g * 4 <= fetch_list[w, h, g] // 64 < (g + 1) * 4. partners[w, h, g, :] are 2 different blocks stored by index h of gx, none equal to fetch_list[w, h, g] // 64.
All inputs are finite; a program needn't handle non-finite values.
Results may differ from a plain program's by a relative error of at most 0.0003.
Values may be sent and summed in bfloat16 or wider, within the bound.
A program may use at most 192 MiB of HBM per device.

v0:
```python
import jax
import jax.numpy as jnp
from jax import lax
from jax.sharding import PartitionSpec as P

SLICE = 8


EPS = 1e-06


def normalize(source):
    values = source.astype(jnp.float32)
    return (values * lax.rsqrt(jnp.sum(values * values, axis=-1, keepdims=True) + EPS)).astype(
        jnp.bfloat16
    )


def dense_tiles(arrived, row_valid, chosen, owned_full, col_valid):
    slots, lent_rows, width = arrived.shape
    owned, block, _ = owned_full.shape
    flat_rows = arrived.reshape(slots * lent_rows, width)
    listed = jnp.any(
        chosen[:, :, None] == jnp.arange(owned, dtype=jnp.int32)[None, None, :], axis=1
    )
    listed_pairs = jnp.transpose(listed.reshape(slots, owned // 2, 2), (1, 0, 2))
    column_pairs = owned_full.reshape(owned // 2, 2, block, width)
    valid_pairs = col_valid.reshape(owned // 2, 2, block)

    def advance(best_rows, entries):
        columns, picked, valid_cols = entries
        scores = jnp.einsum("rd,cbd->rcb", flat_rows, columns, preferred_element_type=jnp.float32)
        scores = scores.reshape(slots, lent_rows, 2, block)
        keep = row_valid[:, :, None, None] & picked[:, None, :, None] & valid_cols[None, None, :, :]
        scores = jnp.where(keep, scores, jnp.float32(-1.0))
        return (jnp.maximum(best_rows, jnp.max(scores, axis=(2, 3))), jnp.max(scores, axis=(0, 1)))

    start = jnp.full((slots, lent_rows), -1.0, jnp.float32)
    best_rows, col_parts = lax.scan(advance, start, (column_pairs, listed_pairs, valid_pairs))
    return (best_rows, col_parts.reshape(owned, block))


def on_device(embeds, fetch_list, partners, counts):
    owned, quarter, width = embeds.shape
    slice_rows = SLICE
    pieces = quarter // slice_rows
    my_group = lax.axis_index("gx")
    my_lane = lax.axis_index("gy")
    block = quarter * lax.axis_size("gy")
    first = my_group * owned
    waves = fetch_list.shape[0]
    own_unit = normalize(embeds)
    own_pieces = own_unit.reshape(owned, pieces, slice_rows, width)
    owned_full = lax.all_gather(own_unit, "gy", axis=1, tiled=True)
    positions = jnp.arange(block, dtype=jnp.int32)
    own_counts = lax.dynamic_slice_in_dim(counts, first, owned)
    col_valid = positions[None, :] < own_counts[:, None]
    row_positions = my_lane * quarter + jnp.arange(quarter, dtype=jnp.int32)
    slice_offsets = my_lane * quarter + jnp.arange(slice_rows, dtype=jnp.int32)
    local_ids = jnp.arange(owned, dtype=jnp.int32)
    piece_ids = jnp.arange(pieces, dtype=jnp.int32)
    row_total = jnp.full((owned, quarter), -1.0, jnp.float32)
    col_total = jnp.full((owned, block), -1.0, jnp.float32)
    for wave_index in range(waves):
        tiles = lax.dynamic_index_in_dim(fetch_list[wave_index], my_group, 1, False)
        outgoing_sent_block = tiles // pieces - first
        outgoing_sent_piece = tiles % pieces
        outbound = own_pieces[outgoing_sent_block, outgoing_sent_piece]
        arrived = lax.all_to_all(outbound, "gx", split_axis=0, concat_axis=0, tiled=True)
        incoming = lax.dynamic_index_in_dim(fetch_list[wave_index], my_group, 0, False)
        arrived_counts = counts[incoming // pieces]
        arrived_rows = (incoming % pieces)[:, None] * slice_rows + slice_offsets[None, :]
        row_valid = arrived_rows < arrived_counts[:, None]
        chosen = lax.dynamic_index_in_dim(partners[wave_index], my_group, 0, False) - first
        row_best, col_best = dense_tiles(arrived, row_valid, chosen, owned_full, col_valid)
        returned = lax.all_to_all(row_best, "gx", split_axis=0, concat_axis=0, tiled=True)
        match = (outgoing_sent_block[:, None, None] == local_ids[None, :, None]) & (
            outgoing_sent_piece[:, None, None] == piece_ids[None, None, :]
        )
        placed = jnp.max(
            jnp.where(match[:, :, :, None], returned[:, None, None, :], jnp.float32(-1.0)), axis=0
        )
        row_total = jnp.maximum(row_total, placed.reshape(owned, quarter))
        col_total = jnp.maximum(col_total, col_best)
    col_all = lax.pmax(col_total, "gy")
    col_mine = lax.dynamic_slice_in_dim(col_all, my_lane * quarter, quarter, 1)
    nearest = jnp.maximum(row_total, col_mine)
    mine_valid = row_positions[None, :] < own_counts[:, None]
    return jnp.where(mine_valid, nearest, jnp.float32(-1.0))


def solution(mesh):
    in_specs = (P("gx", "gy", None), P(), P(), P())
    out_specs = P("gx", "gy")
    return jax.shard_map(
        on_device, mesh=mesh, in_specs=in_specs, out_specs=out_specs, check_vma=False
    )
```

profile of v0, /device:TPU:0, one launch (start us, length us, event | category | flops | bytes accessed | tf_op | source)
XLA Modules:
  0.0 160.2 jit_solution(2294895422547656017)
XLA Ops:
  6.5 2.7 %fusion.26 = f32[4,512]{1,0:T(4,128)S(1)} fusion(bf16[4,512,768]{2,1,0:T(8,128)(2,1)} %param.8), kind=kLoop, calls=%fused_computation.34 | loop fusion | flops 4716544 | bytes 3153920 | tf_op jit(solution)/shard_map/reduce_sum | solution.py:14
  9.3 4.1 %fusion.27 = bf16[4,512,768]{2,1,0:T(8,128)(2,1)} fusion(bf16[4,512,768]{2,1,0:T(8,128)(2,1)} %param.8, f32[4,512]{1,0:T(4,128)S(1)} %add_rsqrt_fusion), kind=kLoop, calls=%fused_computation.35 | loop fusion | flops 4718592 | bytes 6299648 | tf_op jit(solution)/shard_map/convert_element_type | solution.py:14
  13.7 2.2 %fusion.58 = bf16[4,64,8,768]{3,2,1,0:T(8,128)(2,1)} fusion(f32[4,512]{1,0:T(4,128)S(1)} %add_rsqrt_fusion, bf16[4,512,768]{2,1,0:T(8,128)(2,1)S(1)} %copy-done.1), kind=kLoop, calls=%fused_computation.135 | loop fusion | flops 4718592 | bytes 6299648 | tf_op jit(solution)/shard_map/reshape | solution.py:53
  16.0 3.1 %gather_fusion.3 = bf16[8,8,768]{2,1,0:T(8,128)(2,1)} fusion(bf16[4,64,8,768]{3,2,1,0:T(8,128)(2,1)} %fusion.58, s32[8]{0:T(128)S(1)} %fusion.50), kind=kCustom, calls=%fused_computation.3 | custom fusion | bytes 196672 | tf_op jit(solution)/shard_map/gather | solution.py:68
  19.0 7.3 %all-to-all-start.2 = ((bf16[8,8,768]{2,1,0:T(8,128)(2,1)}), bf16[8,8,768]{2,1,0:T(8,128)(2,1)S(1)}, u32[]{:S(2)}, u32[]{:S(2)}) async-start(bf16[8,8,768]{2,1,0:T(8,128)(2,1)} %gather_fusion.3), calls=%async_computation.2 | async-start | bytes 196608 | tf_op jit(solution)/shard_map/all_to_all | solution.py:69
  26.8 0.6 gather_fusion.2
  27.5 3.6 %gather_fusion.1 = bf16[8,8,768]{2,1,0:T(8,128)(2,1)} fusion(bf16[4,64,8,768]{3,2,1,0:T(8,128)(2,1)} %fusion.58, s32[8]{0:T(128)S(1)} %fusion.51), kind=kCustom, calls=%fused_computation.1 | custom fusion | bytes 196672 | tf_op jit(solution)/shard_map/gather | solution.py:68
  31.1 0.6 gather_fusion
  32.4 1.1 all-to-all-done.2
  33.4 5.0 %all-to-all-start = ((bf16[8,8,768]{2,1,0:T(8,128)(2,1)}), bf16[8,8,768]{2,1,0:T(8,128)(2,1)S(1)}, u32[]{:S(2)}, u32[]{:S(2)}) async-start(bf16[8,8,768]{2,1,0:T(8,128)(2,1)} %gather_fusion.1), calls=%async_computation | async-start | bytes 196608 | tf_op jit(solution)/shard_map/all_to_all | solution.py:69
  38.4 60.0 %all-gather.2.cloned.1.call-done = bf16[4,2048,768]{2,1,0:T(8,128)(2,1)} async-done(((bf16[4,512,768]{2,1,0:T(8,128)(2,1)}), bf16[4,2048,768]{2,1,0:T(8,128)(2,1)}) %all-gather.2.cloned.1.call-update) | async-done | bytes 12582928 | tf_op jit(solution)/shard_map/all_gather | solution.py:54
  98.4 12.7 %while.27 = (s32[]{:T(128)}, f32[8,8]{1,0:T(8,128)}, f32[2,2,2048]{2,1,0:T(2,128)S(1)}, pred[2,8,2]{1,2,0:T(4,128)(4,1)S(1)}, pred[2,2,2048]{2,1,0:T(4,128)(4,1)...) while((s32[]{:T(128)}, f32[8,8]{1,0:T(8,128)}, ...), condition=%wide.region_11.12_spmd.clone, body=%wide.region_8.11_spmd.clone.sunk | while | flops 403697984 | bytes 6454055 | solution.py:39
  98.8 4.9 %fusion.62 = (f32[2,2048]{1,0:T(2,128)S(1)}, f32[64]{0:T(128)S(1)}) fusion(bf16[64,768]{1,0:T(8,128)(2,1)S(1)} %get-tuple-element.389, bf16[2,2,2048,768]{3,2,1,0:T(8,128)(2,1)} %get-tuple-element.388, s32[]{:T(128)S(6)} %copy.21, pred[2,2048]{1,0:T(4,128)(4,1)S(1)} %dynamic-slice_bitcast_fusion.10, pred[64,2]{0,1:T(4,128)(4,1)S(1)} %broadcast_and_fusion.7), kind=kOutput, calls=%fused_computation.132.clone.1 | convolution fusion | flops 403697600 | bytes 6410628 | tf_op jit(solution)/shard_map/while/body/eval_jaxpr/rd,cbd->rcb/dot_general | solution.py:32
  104.8 4.9 %fusion.62 = (f32[2,2048]{1,0:T(2,128)S(1)}, f32[64]{0:T(128)S(1)}) fusion(bf16[64,768]{1,0:T(8,128)(2,1)S(1)} %get-tuple-element.389, bf16[2,2,2048,768]{3,2,1,0:T(8,128)(2,1)} %get-tuple-element.388, s32[]{:T(128)S(6)} %copy.21, pred[2,2048]{1,0:T(4,128)(4,1)S(1)} %dynamic-slice_bitcast_fusion.10, pred[64,2]{0,1:T(4,128)(4,1)S(1)} %broadcast_and_fusion.7), kind=kOutput, calls=%fused_computation.132.clone.1 | convolution fusion | flops 403697600 | bytes 6410628 | tf_op jit(solution)/shard_map/while/body/eval_jaxpr/rd,cbd->rcb/dot_general | solution.py:32
  109.8 1.3 select_maximum_fusion.5
  111.1 5.5 %all-to-all-start.3 = ((f32[8,1,8]{2,1,0:T(1,128)}), f32[8,1,8]{2,1,0:T(1,128)S(1)}, u32[]{:S(2)}, u32[]{:S(2)}) async-start(f32[8,1,8]{2,1,0:T(1,128)} %bitcast.20), calls=%async_computation.3 | async-start | bytes 8192 | tf_op jit(solution)/shard_map/all_to_all | solution.py:76
  116.7 12.7 %while.26 = (s32[]{:T(128)}, f32[8,8]{1,0:T(8,128)}, f32[2,2,2048]{2,1,0:T(2,128)S(1)}, pred[2,8,2]{1,2,0:T(4,128)(4,1)S(1)}, pred[2,2,2048]{2,1,0:T(4,128)(4,1)...) while((s32[]{:T(128)}, f32[8,8]{1,0:T(8,128)}, ...), condition=%wide.region_5.6_spmd.clone, body=%wide.region_2.5_spmd.clone.sunk | while | flops 403697984 | bytes 6454055 | solution.py:39
  117.1 4.9 %fusion.61 = (f32[2,2048]{1,0:T(2,128)S(1)}, f32[64]{0:T(128)S(1)}) fusion(bf16[64,768]{1,0:T(8,128)(2,1)S(1)} %get-tuple-element.425, bf16[2,2,2048,768]{3,2,1,0:T(8,128)(2,1)} %get-tuple-element.424, s32[]{:T(128)S(6)} %copy.30, pred[2,2048]{1,0:T(4,128)(4,1)S(1)} %dynamic-slice_bitcast_fusion.8, pred[64,2]{0,1:T(4,128)(4,1)S(1)} %broadcast_and_fusion.6), kind=kOutput, calls=%fused_computation.131.clone.1 | convolution fusion | flops 403697600 | bytes 6410628 | tf_op jit(solution)/shard_map/while/body/eval_jaxpr/rd,cbd->rcb/dot_general | solution.py:32
  123.1 4.9 %fusion.61 = (f32[2,2048]{1,0:T(2,128)S(1)}, f32[64]{0:T(128)S(1)}) fusion(bf16[64,768]{1,0:T(8,128)(2,1)S(1)} %get-tuple-element.425, bf16[2,2,2048,768]{3,2,1,0:T(8,128)(2,1)} %get-tuple-element.424, s32[]{:T(128)S(6)} %copy.30, pred[2,2048]{1,0:T(4,128)(4,1)S(1)} %dynamic-slice_bitcast_fusion.8, pred[64,2]{0,1:T(4,128)(4,1)S(1)} %broadcast_and_fusion.6), kind=kOutput, calls=%fused_computation.131.clone.1 | convolution fusion | flops 403697600 | bytes 6410628 | tf_op jit(solution)/shard_map/while/body/eval_jaxpr/rd,cbd->rcb/dot_general | solution.py:32
  128.0 1.3 select_maximum_fusion.4
  129.4 10.4 %pmax.7 = f32[4,2048]{1,0:T(4,128)S(1)} all-reduce(f32[4,2048]{1,0:T(4,128)S(1)} %max.26), channel_id=1, replica_groups=mesh['gx'=8,'gy'=4] {'gy'}, use_global_device_ids=true, to_apply=%region_13.14 | all-reduce | flops 8192 | bytes 65536 | tf_op jit(solution)/shard_map/pmax | solution.py:85
  139.9 6.0 %all-to-all-start.1 = ((f32[8,1,8]{2,1,0:T(1,128)}), f32[8,1,8]{2,1,0:T(1,128)S(1)}, u32[]{:S(2)}, u32[]{:S(2)}) async-start(f32[8,1,8]{2,1,0:T(1,128)} %bitcast.10), calls=%async_computation.1 | async-start | bytes 8192 | tf_op jit(solution)/shard_map/all_to_all | solution.py:76
  146.0 6.4 %all-to-all-done.1 = f32[8,1,8]{2,1,0:T(1,128)S(1)} async-done(((f32[8,1,8]{2,1,0:T(1,128)}), f32[8,1,8]{2,1,0:T(1,128)S(1)}, u32[]{:S(2)}, u32[]{:S(2)}) %all-to-all-start.1) | async-done | bytes 288 | tf_op jit(solution)/shard_map/all_to_all | solution.py:76
  152.7 0.7 maximum_select_fusion
  (90 shorter events, 4.8 us)
Async XLA Ops:
  6.5 7.2 %copy-start.1 = (bf16[4,512,768]{2,1,0:T(8,128)(2,1)S(1)}, bf16[4,512,768]{2,1,0:T(8,128)(2,1)}, u32[]{:S(2)}) copy-start(bf16[4,512,768]{2,1,0:T(8,128)(2,1)} %param.8) | copy-start | bytes 9437188
  6.5 6.9 %copy-start.3 = (s32[2,8,8]{2,1,0:T(8,128)S(1)}, s32[2,8,8]{2,1,0:T(8,128)}, u32[]{:S(2)}) copy-start(s32[2,8,8]{2,1,0:T(8,128)} %param.9) | copy-start | bytes 1540
  6.5 91.9 %all-gather.2.cloned.1.call-start = ((), (), s32[]{:S(2)}) async-start(), calls=%async_computation.4 | async-start | bytes 15728640 | tf_op jit(solution)/shard_map/all_gather | solution.py:54
  13.4 12.9 %copy-start.2 = (s32[2,8,8,2]{2,3,1,0:T(2,128)S(1)}, s32[2,8,8,2]{2,3,1,0:T(2,128)}, u32[]{:S(2)}) copy-start(s32[2,8,8,2]{2,3,1,0:T(2,128)} %param.10) | copy-start | bytes 3076
  13.4 13.0 %copy-start = (s32[32]{0:T(128)S(1)}, s32[32]{0:T(128)}, u32[]{:S(2)}) copy-start(s32[32]{0:T(128)} %param.11) | copy-start | bytes 388
  19.0 14.4 %all-to-all-start.2 = ((bf16[8,8,768]{2,1,0:T(8,128)(2,1)}), bf16[8,8,768]{2,1,0:T(8,128)(2,1)S(1)}, u32[]{:S(2)}, u32[]{:S(2)}) async-start(bf16[8,8,768]{2,1,0:T(8,128)(2,1)} %gather_fusion.3), calls=%async_computation.2 | async-start | bytes 196608 | tf_op jit(solution)/shard_map/all_to_all | solution.py:69
  33.4 77.7 %all-to-all-start = ((bf16[8,8,768]{2,1,0:T(8,128)(2,1)}), bf16[8,8,768]{2,1,0:T(8,128)(2,1)S(1)}, u32[]{:S(2)}, u32[]{:S(2)}) async-start(bf16[8,8,768]{2,1,0:T(8,128)(2,1)} %gather_fusion.1), calls=%async_computation | async-start | bytes 196608 | tf_op jit(solution)/shard_map/all_to_all | solution.py:69
  111.1 28.7 %all-to-all-start.3 = ((f32[8,1,8]{2,1,0:T(1,128)}), f32[8,1,8]{2,1,0:T(1,128)S(1)}, u32[]{:S(2)}, u32[]{:S(2)}) async-start(f32[8,1,8]{2,1,0:T(1,128)} %bitcast.20), calls=%async_computation.3 | async-start | bytes 8192 | tf_op jit(solution)/shard_map/all_to_all | solution.py:76
  139.9 12.5 %all-to-all-start.1 = ((f32[8,1,8]{2,1,0:T(1,128)}), f32[8,1,8]{2,1,0:T(1,128)S(1)}, u32[]{:S(2)}, u32[]{:S(2)}) async-start(f32[8,1,8]{2,1,0:T(1,128)} %bitcast.10), calls=%async_computation.1 | async-start | bytes 8192 | tf_op jit(solution)/shard_map/all_to_all | solution.py:76
Sparse Core Ops, SparseCore 0:
  13.6 84.7 all-gather.1
where the time goes:
time: 161 us; the launch traced here: 160 us
  waiting for transfers between devices  67.4 us (42%)
  starting transfers between devices  23.8 us (15%)
  matrix products  19.7 us (12%)
  other arithmetic  14.9 us (9%)
  between operations  13.6 us (8%)
  blocking collectives  10.4 us (6%)
  local copies, waits for them, and re-layouts  10.3 us (6%)
    all_gather x1, waiting for transfers between devices, on_device(): owned_full = lax.all_gather(own_unit, 'gy', axis=1, tiled=True)  60 us
    dot_general x4, matrix products, advance(): jnp.einsum('rd,cbd->rcb', flat_rows, columns, preferred_element_type=jnp....  19.7 us
    all_to_all x2, starting transfers between devices, on_device(): lax.all_to_all(outbound, 'gx', split_axis=0, concat_axis=0, tiled=True)  12.3 us
    all_to_all x2, starting transfers between devices, on_device(): lax.all_to_all(row_best, 'gx', split_axis=0, concat_axis=0, tiled=True)  11.5 us
    pmax x1, blocking collectives, on_device(): col_all = lax.pmax(col_total, 'gy')  10.4 us
    gather x2, local copies, waits for them, and re-layouts, on_device(): outbound = own_pieces[outgoing_sent_block, outgoing_sent_piece]  6.7 us
    all_to_all x2, waiting for transfers between devices, on_device(): lax.all_to_all(row_best, 'gx', split_axis=0, concat_axis=0, tiled=True)  6.37 us
    convert_element_type x1, other arithmetic, normalize(): (values * lax.rsqrt(jnp.sum(values * values, axis=-1, keepdims=True) + EP...  4.14 us
  transfers between devices with their start and end apart: 5, of which 3 were waited for; matrix products, arithmetic and copies ran while one was open for 23% of the time, Pallas kernels for 0%

commit v1 on v0

v1 whole, which is shorter than its diff:
```python
import functools

import jax
import jax.numpy as jnp
from jax import lax
from jax.experimental import pallas as pl
from jax.experimental.pallas import tpu as pltpu
from jax.sharding import PartitionSpec as P

SLICE = 8
LANES = 128
STEP = 256
EPS = 1e-06
MESH = pl.DeviceIdType.MESH


def unit_rows(values):
    return values * lax.rsqrt(jnp.sum(values * values, axis=-1, keepdims=True) + EPS)


def kernel(
    shape,
    emb_hbm, fetch_hbm, part_hbm, cnt_hbm, out_ref,
    emb, unit, stage, tiles, colacc, rpart, rin, rsum, qin, vecs, fetch, part, cnt,
    load_sem, list_sem,
    send1, recv1, sendx, recvx, sendc, recvc, sendd, recvd, sendr, recvr, sendq, recvq,
):
    groups, owned, quarter, waves = shape
    pieces = quarter // SLICE
    per = waves * SLICE
    own_rows = owned * quarter
    in_tile = LANES // per
    chunks = groups // in_tile
    cs = groups // 8
    me = lax.axis_index("gx")
    lane = lax.axis_index("gy")
    core = lane + 1 - 2 * lax.rem(lane, 2)
    far = lax.rem(lane + 2, 4)
    diag = 3 - lane
    first = me * owned

    loads = []
    for b in range(owned):
        rows = pl.ds(b * quarter // 16, quarter // 16)
        loads.append(pltpu.make_async_copy(emb_hbm.at[rows], emb.at[rows], load_sem.at[b]))
    lists = [
        pltpu.make_async_copy(fetch_hbm, fetch, list_sem.at[0]),
        pltpu.make_async_copy(part_hbm, part, list_sem.at[1]),
        pltpu.make_async_copy(cnt_hbm, cnt, list_sem.at[2]),
    ]
    for copy in lists + loads:
        copy.start()

    barrier = pltpu.get_barrier_semaphore()
    for k in range(1, groups):
        pl.semaphore_signal(
            barrier, inc=1, device_id=(lax.rem(me + k, groups), lane), device_id_type=MESH
        )
    for other in (core, far, diag):
        pl.semaphore_signal(barrier, inc=1, device_id=(me, other), device_id_type=MESH)

    for copy in lists + loads:
        copy.wait()

    def lent(h):
        halves = []
        for w in range(waves):
            local = fetch[w, h, me] - first * pieces
            local = jnp.clip(local, 0, owned * pieces - 1)
            pair = lax.div(local, 2)
            both = emb[pair].astype(jnp.float32)
            odd = jnp.full((SLICE, emb.shape[2]), local - 2 * pair, jnp.int32) == 1
            halves.append(jnp.where(odd, both[SLICE:], both[:SLICE]))
        return unit_rows(jnp.concatenate(halves, axis=0)).astype(jnp.bfloat16)

    def span(g, count=1):
        return pl.ds(pl.multiple_of(g * per, per), count * per)

    def out1(h):
        return pltpu.make_async_remote_copy(
            src_ref=stage.at[span(h)],
            dst_ref=tiles.at[lane, span(me)],
            send_sem=send1.at[h],
            recv_sem=recv1.at[me],
            device_id=(h, lane),
            device_id_type=MESH,
        )

    def in1(g):
        return pltpu.make_async_remote_copy(
            src_ref=stage.at[span(g)],
            dst_ref=tiles.at[lane, span(g)],
            send_sem=send1.at[g],
            recv_sem=recv1.at[g],
            device_id=(g, lane),
            device_id_type=MESH,
        )

    def hop(source, target, c, send, recv):
        part_of = tiles.at[source, span(c * cs, cs)]
        return pltpu.make_async_remote_copy(
            src_ref=part_of,
            dst_ref=part_of,
            send_sem=send.at[c],
            recv_sem=recv.at[c],
            device_id=(me, target),
            device_id_type=MESH,
        )

    for k in range(1, groups):
        h = lax.rem(me + k, groups)
        stage[span(h), :] = lent(h)
        if k == 1:
            pl.semaphore_wait(barrier, groups + 2)
        out1(h).start()
    tiles[lane, span(me), :] = lent(me)

    col = lax.broadcasted_iota(jnp.int32, (8, LANES), 1)
    slot = col // SLICE
    for c in range(chunks):
        limit = jnp.zeros((8, LANES), jnp.int32)
        left = jnp.zeros((8, LANES), jnp.int32)
        right = jnp.zeros((8, LANES), jnp.int32)
        for i in range(in_tile):
            g = c * in_tile + i
            for w in range(waves):
                t = fetch[w, me, g]
                here = slot == i * waves + w
                bound = cnt[lax.div(t, pieces)] - lax.rem(t, pieces) * SLICE
                limit = jnp.where(here, bound, limit)
                left = jnp.where(here, part[w, me, 0, g] - first, left)
                right = jnp.where(here, part[w, me, 1, g] - first, right)
        vecs[c, 0] = limit - lax.rem(col, SLICE)
        vecs[c, 1] = left
        vecs[c, 2] = right

    rows_each = 64

    def own(i, carry):
        at = pl.ds(pl.multiple_of(i * rows_each, rows_each), rows_each)
        held = emb[pl.ds(i * (rows_each // 16), rows_each // 16)].astype(jnp.float32)
        unit[at, :] = unit_rows(held.reshape(rows_each, -1)).astype(jnp.bfloat16)
        return carry

    lax.fori_loop(0, own_rows // rows_each, own, 0)

    home = lax.div(me, cs)
    order = [lax.rem(home + 8 - k, 8) for k in range(8)]
    for k, c in enumerate(order):
        for i in range(cs):
            g = c * cs + i
            if cs == 1:
                if k:
                    in1(g).wait_recv()
            else:
                pl.when(g != me)(lambda g=g: in1(g).wait_recv())
        hop(lane, far, c, sendx, recvx).start()
        hop(lane, core, c, sendc, recvc).start()

    def score(la, lb, begin):
        def one(c, carry):
            rows = pl.ds(pl.multiple_of(c * LANES, LANES), LANES)
            tile = jnp.concatenate([tiles[la, rows, :], tiles[lb, rows, :]], axis=0)
            limit, left, right = vecs[c, 0], vecs[c, 1], vecs[c, 2]
            within = jnp.concatenate([limit - la * quarter, limit - lb * quarter], axis=1)
            pick_l = jnp.concatenate([left, left], axis=1)
            pick_r = jnp.concatenate([right, right], axis=1)
            best = jnp.full((8, 2 * LANES), -1.0, jnp.float32)
            for j in range(own_rows // STEP):
                b, offset = divmod(j * STEP, quarter)
                at = pl.ds(j * STEP, STEP)
                s = lax.dot_general(
                    unit[at, :], tile, (((1,), (1,)), ((), ())), preferred_element_type=jnp.float32
                )
                picked = (within > 0) & ((pick_l == b) | (pick_r == b))
                place = lax.broadcasted_iota(jnp.int32, (STEP, 2 * LANES), 0)
                seen = place < cnt[first + b] - lane * quarter - offset
                masked = jnp.where(seen, s, -1.0).reshape(STEP // 8, 8, 2 * LANES)
                best = jnp.maximum(best, jnp.where(picked, jnp.max(masked, axis=0), -1.0))
                s = jnp.where(picked[None], s.reshape(STEP // 8, 8, 2 * LANES), -1.0)
                s = s.reshape(STEP, 2 * LANES)
                s = jnp.maximum(s[:, :LANES], s[:, LANES:])
                if begin and chunks == 1:
                    colacc[at, :] = s
                else:
                    colacc[at, :] = jnp.maximum(colacc[at, :], s)
            rpart[la, c] = best[:, :LANES]
            rpart[lb, c] = best[:, LANES:]
            return carry

        if chunks == 1:
            one(0, 0)
        else:
            lax.fori_loop(0, chunks, one, 0)

    if chunks > 1:
        colacc[...] = jnp.full(colacc.shape, -1.0, jnp.float32)

    def give(target, i):
        return pltpu.make_async_remote_copy(
            src_ref=rpart.at[target],
            dst_ref=rin.at[lane],
            send_sem=sendr.at[i],
            recv_sem=recvr.at[i],
            device_id=(me, target),
            device_id_type=MESH,
        )

    def take(source, i):
        return pltpu.make_async_remote_copy(
            src_ref=rpart.at[source],
            dst_ref=rin.at[source],
            send_sem=sendr.at[i],
            recv_sem=recvr.at[i],
            device_id=(me, source),
            device_id_type=MESH,
        )

    for c in order:
        hop(core, core, c, sendc, recvc).wait_recv()
    score(lane, core, True)
    give(core, 0).start()
    for c in order:
        hop(far, far, c, sendx, recvx).wait_recv()
        hop(far, core, c, sendd, recvd).start()
    for c in order:
        hop(diag, core, c, sendd, recvd).wait_recv()
    score(far, diag, False)
    give(far, 1).start()
    give(diag, 2).start()

    best = rpart[lane]
    for i, other in enumerate((core, far, diag)):
        take(other, i).wait_recv()
        best = jnp.maximum(best, rin[other])
    rsum[...] = best

    def back(g):
        return pltpu.make_async_remote_copy(
            src_ref=rsum.at[lax.div(g, in_tile)],
            dst_ref=qin.at[me],
            send_sem=sendq.at[g],
            recv_sem=recvq.at[me],
            device_id=(g, lane),
            device_id_type=MESH,
        )

    def home_again(h):
        return pltpu.make_async_remote_copy(
            src_ref=rsum.at[lax.div(h, in_tile)],
            dst_ref=qin.at[h],
            send_sem=sendq.at[h],
            recv_sem=recvq.at[h],
            device_id=(h, lane),
            device_id_type=MESH,
        )

    for k in range(1, groups):
        back(lax.rem(me + k, groups)).start()
    qin[me] = rsum[lax.div(me, in_tile)]

    lines = own_rows // LANES
    total = jnp.concatenate(
        [
            jnp.max(colacc[i * LANES:(i + 1) * LANES, :].T, axis=0, keepdims=True)
            for i in range(lines)
        ],
        axis=0,
    )

    for k in range(1, groups):
        home_again(lax.rem(me + groups - k, groups)).wait_recv()

    spot = lax.broadcasted_iota(jnp.int32, (lines, LANES), 0) * (LANES // SLICE)
    spot = spot + lax.broadcasted_iota(jnp.int32, (lines, LANES), 1) // SLICE
    mine = lax.rem(me, in_tile) * waves
    for h0 in range(0, groups, 8):
        rows8 = jnp.max(qin[h0:h0 + 8], axis=1)
        for w in range(waves):
            x = jnp.where(slot == mine + w, rows8, -1.0)
            for shift in (8, 16, 32, 64):
                x = jnp.maximum(x, pltpu.roll(x, shift, 1))
            for i in range(8):
                local = fetch[w, h0 + i, me] - first * pieces
                total = jnp.maximum(total, jnp.where(spot == local, x[i:i + 1], -1.0))

    each = quarter // LANES
    for i in range(lines):
        b, q = divmod(i, each)
        place = lax.broadcasted_iota(jnp.int32, (1, LANES), 1) + (lane * quarter + q * LANES)
        line = jnp.where(place < cnt[first + b], jnp.maximum(total[i:i + 1], -1.0), -1.0)
        out_ref[b:b + 1, q * LANES:(q + 1) * LANES] = line

    for k in range(1, groups):
        h = lax.rem(me + k, groups)
        out1(h).wait_send()
        back(h).wait_send()
    for c in order:
        hop(lane, far, c, sendx, recvx).wait_send()
        hop(lane, core, c, sendc, recvc).wait_send()
        hop(far, core, c, sendd, recvd).wait_send()
    for i, other in enumerate((core, far, diag)):
        give(other, i).wait_send()


def on_device(embeds, fetch_list, partners, counts):
    owned, quarter, width = embeds.shape
    waves, groups, _ = fetch_list.shape
    own_rows = owned * quarter
    per = waves * SLICE
    chunks = groups * per // LANES
    listed = jnp.transpose(partners, (0, 1, 3, 2))
    anywhere = pl.BlockSpec(memory_space=pl.ANY)
    dma = pltpu.SemaphoreType.DMA
    flops = 2 * 4 * groups * per * own_rows * width
    return pl.pallas_call(
        functools.partial(kernel, (groups, owned, quarter, waves)),
        out_shape=jax.ShapeDtypeStruct((owned, quarter), jnp.float32),
        in_specs=[anywhere] * 4,
        out_specs=pl.BlockSpec(memory_space=pltpu.VMEM),
        scratch_shapes=[
            pltpu.VMEM((own_rows // 16, 16, width), jnp.bfloat16),
            pltpu.VMEM((own_rows, width), jnp.bfloat16),
            pltpu.VMEM((groups * per, width), jnp.bfloat16),
            pltpu.VMEM((4, groups * per, width), jnp.bfloat16),
            pltpu.VMEM((own_rows, LANES), jnp.float32),
            pltpu.VMEM((4, chunks, 8, LANES), jnp.float32),
            pltpu.VMEM((4, chunks, 8, LANES), jnp.float32),
            pltpu.VMEM((chunks, 8, LANES), jnp.float32),
            pltpu.VMEM((groups, 8, LANES), jnp.float32),
            pltpu.VMEM((chunks, 3, 8, LANES), jnp.int32),
            pltpu.SMEM(fetch_list.shape, jnp.int32),
            pltpu.SMEM(listed.shape, jnp.int32),
            pltpu.SMEM(counts.shape, jnp.int32),
            dma((owned,)),
            dma((3,)),
            dma((groups,)),
            dma((groups,)),
            dma((8,)),
            dma((8,)),
            dma((8,)),
            dma((8,)),
            dma((8,)),
            dma((8,)),
            dma((3,)),
            dma((3,)),
            dma((groups,)),
            dma((groups,)),
        ],
        compiler_params=pltpu.CompilerParams(
            collective_id=0, has_side_effects=True, vmem_limit_bytes=60 * 2**20
        ),
        cost_estimate=pl.CostEstimate(
            flops=flops, bytes_accessed=own_rows * width * 2, transcendentals=0
        ),
    )(embeds.reshape(own_rows // 16, 16, width), fetch_list, listed, counts)


def solution(mesh):
    in_specs = (P("gx", "gy", None), P(), P(), P())
    out_specs = P("gx", "gy")
    return jax.shard_map(
        on_device, mesh=mesh, in_specs=in_specs, out_specs=out_specs, check_vma=False
    )
```

time: 161 us -> 27.4 us (0.17)
  waiting for transfers between devices: 67.4 us -> 0 us
  Pallas kernels: 0 us -> 25.9 us
  starting transfers between devices: 23.8 us -> 0 us
  matrix products: 19.7 us -> 0 us
  other arithmetic: 14.9 us -> 0 us
  between operations: 13.6 us -> 0.01 us
  blocking collectives: 10.4 us -> 0 us
  local copies, waits for them, and re-layouts: 10.3 us -> 1.3 us
    all_gather x1 -> x0, waiting for transfers between devices: 60 us -> none  [on_device(): owned_full = lax.all_gather(own_unit, 'gy', axis=1, tiled=True)]
    pallas_call x0 -> x1, Pallas kernels: none -> 25.9 us  [on_device(): pl.pallas_call(functools.partial(kernel, (groups, owned, quarter, waves))...]
    all_to_all x4 -> x0, starting transfers between devices: 23.8 us -> none  [the longest x2 12.3 us: on_device(): lax.all_to_all(outbound, 'gx', split_axis=0, concat_axis=0, tiled=True)]
    dot_general x4 -> x0, matrix products: 19.7 us -> none  [advance(): jnp.einsum('rd,cbd->rcb', flat_rows, columns, preferred_element_type=jnp....]
    pmax x1 -> x0, blocking collectives: 10.4 us -> none  [on_device(): col_all = lax.pmax(col_total, 'gy')]
    gather x4 -> x0, local copies, waits for them, and re-layouts: 7.99 us -> none  [the longest x2 6.7 us: on_device(): outbound = own_pieces[outgoing_sent_block, outgoing_sent_piece]]
    all_to_all x4 -> x0, waiting for transfers between devices: 7.43 us -> none  [the longest x2 6.37 us: on_device(): lax.all_to_all(row_best, 'gx', split_axis=0, concat_axis=0, tiled=True)]
    convert_element_type x1 -> x0, other arithmetic: 4.14 us -> none  [normalize(): (values * lax.rsqrt(jnp.sum(values * values, axis=-1, keepdims=True) + EP...]
  transfers between devices with their start and end apart: 5 -> 0, of which waited for: 3 -> 0; matrix products, arithmetic and copies ran while one was open for 23% -> 0% of each run, Pallas kernels for 0% -> 0%
where the time goes in v1:
time: 27.4 us; the launch traced here: 27.2 us
  Pallas kernels  25.9 us (95%)
  local copies, waits for them, and re-layouts  1.3 us (5%)
    pallas_call x1, Pallas kernels, on_device(): pl.pallas_call(functools.partial(kernel, (groups, owned, quarter, waves))...  25.9 us
    unnamed x1, local copies, waits for them, and re-layouts  1.3 us

profile of v1, /device:TPU:0, one launch (start us, length us, event | category | flops | bytes accessed | tf_op | source)
XLA Modules:
  0.0 27.2 jit_solution(8213838362834938024)
XLA Ops:
  0.0 25.9 %shard_map.46 = f32[4,512]{1,0:T(4,128)} custom-call(bf16[128,16,768]{2,1,0:T(8,128)(2,1)} %bitcast.2, s32[2,8,8]{2,1,0:T(8,128)} %fetch_hbm.1, s32[2,8,2,8]{3,2,1,0:T(2,128)} %bitcast.3, s32[32]{0:T(128)} %cnt_hbm.1), custom_call_target="tpu_custom_call" | custom-call | flops 1610612736 | bytes 3145728 | tf_op jit(solution)/shard_map/pallas_call | solution.py:316
  25.9 1.3 %copy.6 = f32[4,512]{1,0:T(4,128)} copy(f32[4,512]{1,0:T(4,128)} %shard_map.46) | data formatting | bytes 16384

commit v2 on v1

--- a/solution.py
+++ b/solution.py
@@ -21,9 +21,9 @@
 def kernel(
     shape,
     emb_hbm, fetch_hbm, part_hbm, cnt_hbm, out_ref,
-    emb, unit, stage, tiles, colacc, rpart, rin, rsum, qin, vecs, fetch, part, cnt,
+    emb, unit, stage, tiles, colacc, rpart, qin, vecs, fetch, part, cnt,
     load_sem, list_sem,
-    send1, recv1, sendx, recvx, sendc, recvc, sendd, recvd, sendr, recvr, sendq, recvq,
+    send1, recv1, sendx, recvx, sendc, recvc, sendd, recvd, sendr, recvr, sendn, recvn,
 ):
     groups, owned, quarter, waves = shape
     pieces = quarter // SLICE
@@ -52,12 +52,12 @@
         copy.start()
 
     barrier = pltpu.get_barrier_semaphore()
-    for k in range(1, groups):
-        pl.semaphore_signal(
-            barrier, inc=1, device_id=(lax.rem(me + k, groups), lane), device_id_type=MESH
-        )
-    for other in (core, far, diag):
-        pl.semaphore_signal(barrier, inc=1, device_id=(me, other), device_id_type=MESH)
+    for k in range(groups):
+        for other in (lane, core, far, diag):
+            if k or other is not lane:
+                pl.semaphore_signal(
+                    barrier, inc=1, device_id=(lax.rem(me + k, groups), other), device_id_type=MESH
+                )
 
     for copy in lists + loads:
         copy.wait()
@@ -111,7 +111,7 @@
         h = lax.rem(me + k, groups)
         stage[span(h), :] = lent(h)
         if k == 1:
-            pl.semaphore_wait(barrier, groups + 2)
+            pl.semaphore_wait(barrier, 4 * groups - 1)
         out1(h).start()
     tiles[lane, span(me), :] = lent(me)
 
@@ -184,6 +184,7 @@
                     colacc[at, :] = s
                 else:
                     colacc[at, :] = jnp.maximum(colacc[at, :], s)
+            best = jnp.broadcast_to(jnp.max(best, axis=0, keepdims=True), best.shape)
             rpart[la, c] = best[:, :LANES]
             rpart[lb, c] = best[:, LANES:]
             return carry
@@ -196,68 +197,60 @@
     if chunks > 1:
         colacc[...] = jnp.full(colacc.shape, -1.0, jnp.float32)
 
-    def give(target, i):
-        return pltpu.make_async_remote_copy(
-            src_ref=rpart.at[target],
-            dst_ref=rin.at[lane],
-            send_sem=sendr.at[i],
-            recv_sem=recvr.at[i],
-            device_id=(me, target),
-            device_id_type=MESH,
-        )
-
-    def take(source, i):
-        return pltpu.make_async_remote_copy(
-            src_ref=rpart.at[source],
-            dst_ref=rin.at[source],
-            send_sem=sendr.at[i],
-            recv_sem=recvr.at[i],
-            device_id=(me, source),
-            device_id_type=MESH,
-        )
+    def answer(g, target):
+        at = lax.div(me, 8), pl.ds(lax.rem(me, 8), 1)
+        send = sendn.at[g] if target is lane else sendr.at[target]
+        recv = recvn.at[me] if target is lane else recvr.at[lane]
+        return pltpu.make_async_remote_copy(
+            src_ref=rpart.at[target, lax.div(g, in_tile), pl.ds(0, 1)],
+            dst_ref=qin.at[(lane, *at)],
+            send_sem=send,
+            recv_sem=recv,
+            device_id=(g, target),
+            device_id_type=MESH,
+        )
+
+    def answered(h):
+        return pltpu.make_async_remote_copy(
+            src_ref=rpart.at[lane, lax.div(h, in_tile), pl.ds(0, 1)],
+            dst_ref=qin.at[lane, lax.div(h, 8), pl.ds(lax.rem(h, 8), 1)],
+            send_sem=sendn.at[h],
+            recv_sem=recvn.at[h],
+            device_id=(h, lane),
+            device_id_type=MESH,
+        )
+
+    def all_of(other):
+        return pltpu.make_async_remote_copy(
+            src_ref=rpart.at[other],
+            dst_ref=qin.at[other],
+            send_sem=sendr.at[other],
+            recv_sem=recvr.at[other],
+            device_id=(me, other),
+            device_id_type=MESH,
+        )
+
+    def reply(target):
+        for k in range(1, groups):
+            answer(lax.rem(me + k, groups), target).start()
+        if target is not lane:
+            answer(me, target).start()
 
     for c in order:
         hop(core, core, c, sendc, recvc).wait_recv()
     score(lane, core, True)
-    give(core, 0).start()
+    reply(core)
+    reply(lane)
+    mine_row = rpart[lane, lax.div(me, in_tile), pl.ds(0, 1)]
+    qin[lane, lax.div(me, 8), pl.ds(lax.rem(me, 8), 1)] = mine_row
     for c in order:
         hop(far, far, c, sendx, recvx).wait_recv()
         hop(far, core, c, sendd, recvd).start()
     for c in order:
         hop(diag, core, c, sendd, recvd).wait_recv()
     score(far, diag, False)
-    give(far, 1).start()
-    give(diag, 2).start()
-
-    best = rpart[lane]
-    for i, other in enumerate((core, far, diag)):
-        take(other, i).wait_recv()
-        best = jnp.maximum(best, rin[other])
-    rsum[...] = best
-
-    def back(g):
-        return pltpu.make_async_remote_copy(
-            src_ref=rsum.at[lax.div(g, in_tile)],
-            dst_ref=qin.at[me],
-            send_sem=sendq.at[g],
-            recv_sem=recvq.at[me],
-            device_id=(g, lane),
-            device_id_type=MESH,
-        )
-
-    def home_again(h):
-        return pltpu.make_async_remote_copy(
-            src_ref=rsum.at[lax.div(h, in_tile)],
-            dst_ref=qin.at[h],
-            send_sem=sendq.at[h],
-            recv_sem=recvq.at[h],
-            device_id=(h, lane),
-            device_id_type=MESH,
-        )
-
-    for k in range(1, groups):
-        back(lax.rem(me + k, groups)).start()
-    qin[me] = rsum[lax.div(me, in_tile)]
+    reply(far)
+    reply(diag)
 
     lines = own_rows // LANES
     total = jnp.concatenate(
@@ -269,13 +262,16 @@
     )
 
     for k in range(1, groups):
-        home_again(lax.rem(me + groups - k, groups)).wait_recv()
+        answered(lax.rem(me + groups - k, groups)).wait_recv()
+    for other in (core, far, diag):
+        all_of(other).wait_recv()
 
     spot = lax.broadcasted_iota(jnp.int32, (lines, LANES), 0) * (LANES // SLICE)
     spot = spot + lax.broadcasted_iota(jnp.int32, (lines, LANES), 1) // SLICE
     mine = lax.rem(me, in_tile) * waves
     for h0 in range(0, groups, 8):
-        rows8 = jnp.max(qin[h0:h0 + 8], axis=1)
+        rows8 = jnp.maximum(qin[0, h0 // 8], qin[1, h0 // 8])
+        rows8 = jnp.maximum(rows8, jnp.maximum(qin[2, h0 // 8], qin[3, h0 // 8]))
         for w in range(waves):
             x = jnp.where(slot == mine + w, rows8, -1.0)
             for shift in (8, 16, 32, 64):
@@ -294,13 +290,13 @@
     for k in range(1, groups):
         h = lax.rem(me + k, groups)
         out1(h).wait_send()
-        back(h).wait_send()
+        answered(h).wait_send()
     for c in order:
         hop(lane, far, c, sendx, recvx).wait_send()
         hop(lane, core, c, sendc, recvc).wait_send()
         hop(far, core, c, sendd, recvd).wait_send()
-    for i, other in enumerate((core, far, diag)):
-        give(other, i).wait_send()
+    for other in (core, far, diag):
+        all_of(other).wait_send()
 
 
 def on_device(embeds, fetch_list, partners, counts):
@@ -325,9 +321,7 @@
             pltpu.VMEM((4, groups * per, width), jnp.bfloat16),
             pltpu.VMEM((own_rows, LANES), jnp.float32),
             pltpu.VMEM((4, chunks, 8, LANES), jnp.float32),
-            pltpu.VMEM((4, chunks, 8, LANES), jnp.float32),
-            pltpu.VMEM((chunks, 8, LANES), jnp.float32),
-            pltpu.VMEM((groups, 8, LANES), jnp.float32),
+            pltpu.VMEM((4, groups // 8, 8, LANES), jnp.float32),
             pltpu.VMEM((chunks, 3, 8, LANES), jnp.int32),
             pltpu.SMEM(fetch_list.shape, jnp.int32),
             pltpu.SMEM(listed.shape, jnp.int32),
@@ -342,8 +336,8 @@
             dma((8,)),
             dma((8,)),
             dma((8,)),
-            dma((3,)),
-            dma((3,)),
+            dma((4,)),
+            dma((4,)),
             dma((groups,)),
             dma((groups,)),
         ],

time: 27.4 us -> 26.4 us (0.964)
  Pallas kernels: 25.9 us -> 24.9 us
    pallas_call x1, Pallas kernels: 25.9 us -> 24.9 us  [on_device(): pl.pallas_call(functools.partial(kernel, (groups, owned, quarter, waves))...]
where the time goes in v2:
time: 26.4 us; the launch traced here: 26.2 us
  Pallas kernels  24.9 us (94%)
  local copies, waits for them, and re-layouts  1.3 us (5%)
    pallas_call x1, Pallas kernels, on_device(): pl.pallas_call(functools.partial(kernel, (groups, owned, quarter, waves))...  24.9 us
    unnamed x1, local copies, waits for them, and re-layouts  1.3 us

profile of v2, /device:TPU:0, one launch (start us, length us, event | category | flops | bytes accessed | tf_op | source)
XLA Modules:
  0.0 26.2 jit_solution(17550646185278672728)
XLA Ops:
  0.0 24.9 %shard_map.46 = f32[4,512]{1,0:T(4,128)} custom-call(bf16[128,16,768]{2,1,0:T(8,128)(2,1)} %bitcast.2, s32[2,8,8]{2,1,0:T(8,128)} %fetch_hbm.1, s32[2,8,2,8]{3,2,1,0:T(2,128)} %bitcast.3, s32[32]{0:T(128)} %cnt_hbm.1), custom_call_target="tpu_custom_call" | custom-call | flops 1610612736 | bytes 3145728 | tf_op jit(solution)/shard_map/pallas_call | solution.py:312
  24.9 1.3 %copy.6 = f32[4,512]{1,0:T(4,128)} copy(f32[4,512]{1,0:T(4,128)} %shard_map.46) | data formatting | bytes 16384

commit v3 on v2

--- a/solution.py
+++ b/solution.py
@@ -16,6 +16,10 @@
 
 def unit_rows(values):
     return values * lax.rsqrt(jnp.sum(values * values, axis=-1, keepdims=True) + EPS)
+
+
+def outward(n):
+    return sorted(range(1, n), key=lambda k: (abs(2 * k - n), k))
 
 
 def kernel(
@@ -38,6 +42,7 @@
     far = lax.rem(lane + 2, 4)
     diag = 3 - lane
     first = me * owned
+    far_first = outward(groups)
 
     loads = []
     for b in range(owned):
@@ -54,7 +59,7 @@
     barrier = pltpu.get_barrier_semaphore()
     for k in range(groups):
         for other in (lane, core, far, diag):
-            if k or other is not lane:
+            if (other is lane) != (k == 0):
                 pl.semaphore_signal(
                     barrier, inc=1, device_id=(lax.rem(me + k, groups), other), device_id_type=MESH
                 )
@@ -107,11 +112,11 @@
             device_id_type=MESH,
         )
 
-    for k in range(1, groups):
+    for n, k in enumerate(far_first):
         h = lax.rem(me + k, groups)
         stage[span(h), :] = lent(h)
-        if k == 1:
-            pl.semaphore_wait(barrier, 4 * groups - 1)
+        if n == 0:
+            pl.semaphore_wait(barrier, groups + 2)
         out1(h).start()
     tiles[lane, span(me), :] = lent(me)
 
@@ -145,7 +150,7 @@
     lax.fori_loop(0, own_rows // rows_each, own, 0)
 
     home = lax.div(me, cs)
-    order = [lax.rem(home + 8 - k, 8) for k in range(8)]
+    order = [lax.rem(home + 8 - k, 8) for k in [0, *outward(8)]]
     for k, c in enumerate(order):
         for i in range(cs):
             g = c * cs + i
@@ -231,7 +236,7 @@
         )
 
     def reply(target):
-        for k in range(1, groups):
+        for k in far_first:
             answer(lax.rem(me + k, groups), target).start()
         if target is not lane:
             answer(me, target).start()

time: 26.4 us -> 25 us (0.947)
  Pallas kernels: 24.9 us -> 23.5 us
    pallas_call x1, Pallas kernels: 24.9 us -> 23.5 us  [on_device(): pl.pallas_call(functools.partial(kernel, (groups, owned, quarter, waves))...]
where the time goes in v3:
time: 25 us; the launch traced here: 24.8 us
  Pallas kernels  23.5 us (94%)
  local copies, waits for them, and re-layouts  1.3 us (5%)
    pallas_call x1, Pallas kernels, on_device(): pl.pallas_call(functools.partial(kernel, (groups, owned, quarter, waves))...  23.5 us
    unnamed x1, local copies, waits for them, and re-layouts  1.3 us

profile of v3, /device:TPU:0, one launch (start us, length us, event | category | flops | bytes accessed | tf_op | source)
XLA Modules:
  0.0 24.8 jit_solution(13089805374954582732)
XLA Ops:
  0.0 23.5 %shard_map.46 = f32[4,512]{1,0:T(4,128)} custom-call(bf16[128,16,768]{2,1,0:T(8,128)(2,1)} %bitcast.2, s32[2,8,8]{2,1,0:T(8,128)} %fetch_hbm.1, s32[2,8,2,8]{3,2,1,0:T(2,128)} %bitcast.3, s32[32]{0:T(128)} %cnt_hbm.1), custom_call_target="tpu_custom_call" | custom-call | flops 1610612736 | bytes 3145728 | tf_op jit(solution)/shard_map/pallas_call | solution.py:317
  23.5 1.3 %copy.6 = f32[4,512]{1,0:T(4,128)} copy(f32[4,512]{1,0:T(4,128)} %shard_map.46) | data formatting | bytes 16384
